TPU v7x, 32 devices: a whole 2x2x4 slice. The times are simulated.
32 devices in a mesh: groups: 2 (over y), tm: 16 (over z, x, core), rows: 1.
Axes of the slice: x: 2, y: 2, z: 4, core: 2. Of those that a mesh axis runs over, the one named last changes fastest.
Arguments:
- queries: bfloat16 [32, 4, 64, 1024], P(('groups', 'tm'), 'rows'), parts along dimension 0, may hold values from -60 to 60
- keys: bfloat16 [32, 4, 64, 256], P(('groups', 'tm'), 'rows'), parts along dimension 0, may hold values from -4 to 4
- values: bfloat16 [32, 4, 64, 256], P(('groups', 'tm'), 'rows'), parts along dimension 0, may hold values from -6 to 6
- grad_out: bfloat16 [32, 4, 64, 1024], P(('groups', 'tm'), 'rows'), parts along dimension 0, may hold values from -12 to 12
- frame_mask: int32 [32, 16], P('groups'), parts along dimension 0, may hold values 0 or 1
- clip_frames: int32 [12], P('groups'), parts along dimension 0, may hold values from 1 to 4, 16 in all
- offsets: int32 [24, 2], replicated, may hold values from -3 to 3, as said below
Outputs:
- grad_queries: float32 [32, 4, 64, 1024], P(('groups', 'tm'), 'rows'), parts along dimension 0
- grad_keys: float32 [32, 4, 64, 256], P(('groups', 'tm'), 'rows'), parts along dimension 0
- grad_values: float32 [32, 4, 64, 256], P(('groups', 'tm'), 'rows'), parts along dimension 0
There are 2 independent parts, one for each index of `groups`. A program takes and returns all parts, laid end to end along the dimension named above; an argument that names none is the same for every part. Nothing has to cross between parts.
Inputs may be any that keep to these rules, and one draw needn't show every extreme that they name: `offsets`: row 0 is (0, 0) and row 1 is (0, 1); the rows are distinct cells of the 7 x 7 neighbourhood. `clip_frames`: the lengths sum to 16; the longest clip has exactly 4 frames.
All inputs are finite; a program needn't handle non-finite values.
Results may differ from a plain program's by a relative error of at most 0.005.
Values may be sent and summed in bfloat16 or wider, within the bound.
A program may use at most 128 MiB of HBM per device.

v0:
```python
import jax
import jax.numpy as jnp
from jax import lax
from jax.experimental import pallas as pl
from jax.experimental.pallas import tpu as pltpu
from jax.sharding import PartitionSpec as P

HQ = 8
HK = 2
HD = 128


tile_cols = 8
key_span = 14
negative_big = -1e30


def padded_2(cells, sides, width):
    for axis, dim in sides:
        count = lax.axis_size(axis)
        ends = count - 1
        head = lax.slice_in_dim(cells, 0, width, axis=dim)
        tail = lax.slice_in_dim(cells, cells.shape[dim] - width, cells.shape[dim], axis=dim)
        cells = jnp.concatenate(
            [
                lax.ppermute(tail, axis, [(i, (i + 1) % count) for i in range(ends)]),
                cells,
                lax.ppermute(head, axis, [((i + 1) % count, i) for i in range(ends)]),
            ],
            axis=dim,
        )
    return cells


def passed_along(value, axis, steps):
    count = lax.axis_size(axis)
    pairs = [(source, (source + steps) % count) for source in range(count)]
    return lax.ppermute(value, axis, pairs)


def to_tiles(block, group_size):
    band_rows = block.shape[0]
    count_tiles = block.shape[1] // tile_cols
    shaped = block.reshape(band_rows, count_tiles, tile_cols, HK, group_size, HD)
    shaped = shaped.transpose(1, 3, 4, 0, 2, 5)
    return shaped.reshape(count_tiles, HK, group_size, band_rows * tile_cols, HD)


def from_tiles(tiles, band_rows):
    count_tiles = tiles.shape[0]
    group_size = tiles.shape[2]
    shaped = tiles.reshape(count_tiles, HK, group_size, band_rows, tile_cols, HD)
    shaped = shaped.transpose(3, 0, 4, 1, 2, 5)
    return shaped.reshape(1, band_rows, count_tiles * tile_cols, HK * group_size * HD)


def to_windows(extended):
    ext_rows = extended.shape[1]
    total_width = extended.shape[2]
    padded = jnp.pad(extended, ((0, 0), (0, 0), (3, 3), (0, 0)))
    pieces = [
        padded[:, :, column_tile * tile_cols : column_tile * tile_cols + key_span]
        for column_tile in range(total_width // tile_cols)
    ]
    stacked = jnp.stack(pieces, 0)
    stacked = stacked.reshape(len(pieces), 2, ext_rows, key_span, HK, HD)
    stacked = stacked.transpose(1, 0, 4, 2, 3, 5)
    return stacked.reshape(2, len(pieces), HK, ext_rows * key_span, HD)


def from_windows(window_grads, ext_rows, total_width):
    count_tiles = window_grads.shape[1]
    shaped = window_grads.reshape(2, count_tiles, HK, ext_rows, key_span, HD)
    shaped = shaped.transpose(0, 1, 3, 4, 2, 5).reshape(2, count_tiles, ext_rows, key_span, HK * HD)
    summed = jnp.zeros((2, ext_rows, total_width + 6, HK * HD), jnp.float32)
    for column_tile in range(count_tiles):
        first_col = column_tile * tile_cols
        summed = summed.at[:, :, first_col : first_col + key_span].add(shaped[:, column_tile])
    return summed[:, :, 3 : 3 + total_width]


def spatial_live(offsets, band_rows, total_width):
    ext_rows = band_rows + 6
    count_tiles = total_width // tile_cols
    query_row = jnp.repeat(jnp.arange(band_rows), tile_cols)
    query_col = jnp.tile(jnp.arange(tile_cols), band_rows)
    key_row = jnp.repeat(jnp.arange(ext_rows), key_span)
    key_col = jnp.tile(jnp.arange(key_span), ext_rows)
    delta_row = key_row[None, :] - 3 - query_row[:, None]
    delta_col = key_col[None, :] - 3 - query_col[:, None]
    offset_hit = jnp.any(
        (delta_row[None] == offsets[:, 0, None, None])
        & (delta_col[None] == offsets[:, 1, None, None]),
        axis=0,
    )
    band_index = lax.axis_index("rows")
    image_rows = band_rows * lax.axis_size("rows")
    image_row = band_index * band_rows + key_row - 3
    row_inside = (image_row >= 0) & (image_row < image_rows)
    tile_first = jnp.arange(count_tiles) * tile_cols
    image_col = tile_first[:, None] + key_col[None, :] - 3
    col_inside = (image_col >= 0) & (image_col < total_width)
    return offset_hit[None] & row_inside[None, None] & col_inside[:, None, :]


def running_sum(entries):
    places = jnp.arange(entries.shape[0])
    return jnp.sum(jnp.where(places[None, :] <= places[:, None], entries[None, :], 0), axis=1)


def frame_allowed(frame_mask, clip_frames, distance):
    frames = lax.axis_size("tm")
    lags = min(4, frames)
    own_frame = lax.axis_index("tm")
    seen_frame = (own_frame - distance) % frames
    clip_ends = running_sum(clip_frames)
    clip_starts = clip_ends - clip_frames
    is_longest = (clip_frames == lags).astype(jnp.int32)
    first_longest = (is_longest == 1) & (running_sum(is_longest) == 1)
    rotation = jnp.sum(jnp.where(first_longest, clip_starts, 0))
    own_place = (own_frame + 2 + rotation) % frames
    seen_place = (seen_frame + 2 + rotation) % frames
    own_clip = jnp.sum((own_place >= clip_ends).astype(jnp.int32))
    seen_clip = jnp.sum((seen_place >= clip_ends).astype(jnp.int32))
    grid_rows = jnp.arange(frames)[:, None]
    grid_cols = jnp.arange(frames)[None, :]
    picked = jnp.sum(jnp.where((grid_rows == own_frame) & (grid_cols == seen_frame), frame_mask, 0))
    kept = (picked == 1) | (distance <= 1)
    return (own_clip == seen_clip) & (seen_place <= own_place) & kept


def fold_rims(extended_grads, band_rows):
    interior = extended_grads[:, 3 : 3 + band_rows]
    rim_rows = jnp.concatenate([extended_grads[:, :3], extended_grads[:, band_rows + 3 :]], 1)
    haloed = padded_2(rim_rows.astype(jnp.bfloat16), (("rows", 1),), 3).astype(rim_rows.dtype)
    interior = interior.at[:, :3].add(haloed[:, :3])
    return interior.at[:, band_rows - 3 :].add(haloed[:, 9:])


def body(queries, keys, values, grad_out, frame_mask, clip_frames, offsets):
    band_rows = queries.shape[1]
    total_width = queries.shape[2]
    ext_rows = band_rows + 6
    group_size = HQ // HK
    scale = HD ** (-0.5)
    lags = min(4, lax.axis_size("tm"))
    query_tiles = to_tiles(queries[0], group_size)
    grad_tiles = to_tiles(grad_out[0], group_size)
    spatial = spatial_live(offsets, band_rows, total_width)[:, None, None]
    allowed = [frame_allowed(frame_mask, clip_frames, distance) for distance in range(lags)]
    stacked = jnp.stack([keys[0], values[0]], 0)
    resident = padded_2(stacked, (("rows", 1),), 3)

    def pair_terms(extended):
        windows = to_windows(extended)
        logits = (
            jnp.einsum(
                "cgaqd,cgkd->cgaqk", query_tiles, windows[0], preferred_element_type=jnp.float32
            )
            * scale
        )
        grad_dot = jnp.einsum(
            "cgaqd,cgkd->cgaqk", grad_tiles, windows[1], preferred_element_type=jnp.float32
        )
        return (windows, logits, grad_dot)

    stat_shape = (total_width // tile_cols, HK, group_size, band_rows * tile_cols)
    running = (
        jnp.full(stat_shape, negative_big, jnp.float32),
        jnp.zeros(stat_shape, jnp.float32),
        jnp.zeros(stat_shape, jnp.float32),
    )
    visiting = resident
    visited = []
    for distance in range(lags):
        visited.append(visiting)
        extended = visiting
        live_mask = spatial & allowed[distance]
        run_max, run_sum, run_dot = running
        stat_windows, stat_logits, stat_grad_dot = pair_terms(extended)
        masked = jnp.where(live_mask, stat_logits, negative_big)
        new_max = jnp.maximum(run_max, jnp.max(masked, axis=-1))
        factor = jnp.exp(run_max - new_max)
        weights = jnp.where(live_mask, jnp.exp(stat_logits - new_max[..., None]), 0.0)
        running = (
            new_max,
            run_sum * factor + jnp.sum(weights, axis=-1),
            run_dot * factor + jnp.sum(weights * stat_grad_dot, axis=-1),
        )
        if distance + 1 < lags:
            visiting = passed_along(visiting, "tm", 1)
    log_total = running[0] + jnp.log(running[1])
    mean_grad = running[2] / running[1]
    query_total = jnp.zeros(stat_shape + (HD,), jnp.float32)
    carried = jnp.zeros(resident.shape, jnp.float32)
    visiting = resident
    for distance in range(lags):
        extended = visiting
        live_mask = spatial & allowed[distance]
        grad_windows, grad_logits, grad_grad_dot = pair_terms(extended)
        probs = jnp.where(live_mask, jnp.exp(grad_logits - log_total[..., None]), 0.0)
        probs_low = probs.astype(jnp.bfloat16)
        dscore = (probs * (grad_grad_dot - mean_grad[..., None])).astype(jnp.bfloat16)
        query_part = jnp.einsum(
            "cgaqk,cgkd->cgaqd", dscore, grad_windows[0], preferred_element_type=jnp.float32
        )
        key_part = (
            jnp.einsum("cgaqk,cgaqd->cgkd", dscore, query_tiles, preferred_element_type=jnp.float32)
            * scale
        )
        value_part = jnp.einsum(
            "cgaqk,cgaqd->cgkd", probs_low, grad_tiles, preferred_element_type=jnp.float32
        )
        query_part, window_grads = (query_part, jnp.stack([key_part, value_part], 0))
        query_total = query_total + query_part
        ext_grads = from_windows(window_grads, ext_rows, total_width)
        carried = carried + ext_grads
        if distance + 1 < lags:
            visiting = passed_along(visiting, "tm", 1)
            carried = passed_along(carried, "tm", 1)
    carried = passed_along(carried, "tm", 1 - lags)
    finished = fold_rims(carried, band_rows)
    grad_queries = from_tiles(query_total * scale, band_rows)
    return (grad_queries, finished[0][None], finished[1][None])


MESH = pl.DeviceIdType.MESH
LOG2E = 1.4426950408889634
SCALE = HD**-0.5
GROUP = HQ // HK


def lag_allowed(mask_ref, clip_ref, own_frame, frames, lag):
    clips = clip_ref.shape[0]
    seen_frame = lax.rem(own_frame - lag + frames, frames)
    total = jnp.int32(0)
    rotation = jnp.int32(0)
    found = jnp.int32(0)
    for clip in range(clips):
        length = clip_ref[clip]
        first = jnp.where(length == 4, 1, 0) * (1 - found)
        rotation = rotation + first * total
        found = found + first
        total = total + length
    own_place = own_frame + 2 + rotation
    own_place = jnp.where(own_place >= frames, own_place - frames, own_place)
    own_place = jnp.where(own_place >= frames, own_place - frames, own_place)
    seen_place = seen_frame + 2 + rotation
    seen_place = jnp.where(seen_place >= frames, seen_place - frames, seen_place)
    seen_place = jnp.where(seen_place >= frames, seen_place - frames, seen_place)
    own_clip = jnp.int32(0)
    seen_clip = jnp.int32(0)
    end = jnp.int32(0)
    for clip in range(clips):
        end = end + clip_ref[clip]
        own_clip = own_clip + jnp.where(own_place >= end, 1, 0)
        seen_clip = seen_clip + jnp.where(seen_place >= end, 1, 0)
    kept = jnp.maximum(jnp.where(mask_ref[own_frame, seen_frame] == 1, 1, 0), jnp.where(lag <= 1, 1, 0))
    same = jnp.where(own_clip == seen_clip, 1, 0)
    causal = jnp.where(seen_place <= own_place, 1, 0)
    return kept * same * causal


def fused(
    width, frames,
    mask_ref, clip_ref, offset_ref, query_ref, key_ref, value_ref, cot_ref,
    dq_ref, dk_ref, dv_ref,
    kv, grads, arrived, bias, probs, dots, tops, sums, means, dq_acc, send_sem, recv_sem,
):
    tokens = query_ref.shape[0]
    heads_wide = HK * HD
    own = lax.axis_index("tm")
    core = lax.rem(own, 2)

    def device(step):
        return {"tm": lax.rem(own + step + frames, frames)}

    partner = device(1 - 2 * core)
    ahead, behind = device(2), device(frames - 2)
    far = device(jnp.where(core == 0, frames - 3, 3))
    second_to = device(jnp.where(core == 0, 1, 3))
    second_back = device(jnp.where(core == 0, frames - 3, frames - 1))

    barrier = pltpu.get_barrier_semaphore()
    for peer in (partner, ahead, behind, far):
        pl.semaphore_signal(barrier, inc=1, device_id=peer, device_id_type=MESH)
    kv[0, :, :heads_wide] = key_ref[...]
    kv[0, :, heads_wide:] = value_ref[...]
    pl.semaphore_wait(barrier, 4)

    def remote(index, source, target, peer):
        return pltpu.make_async_remote_copy(
            src_ref=source, dst_ref=target, send_sem=send_sem.at[index], recv_sem=recv_sem.at[index],
            device_id=peer, device_id_type=MESH,
        )

    send_two = remote(0, kv.at[0], kv.at[2], ahead)
    send_one = remote(1, kv.at[0], kv.at[1], second_to)
    relay = remote(2, kv.at[2], kv.at[3], partner)
    send_two.start()
    send_one.start()

    key_id = lax.broadcasted_iota(jnp.int32, (tokens, tokens), 0)
    query_id = lax.broadcasted_iota(jnp.int32, (tokens, tokens), 1)
    delta_col = lax.rem(key_id, width) - lax.rem(query_id, width)
    delta_row = key_id // width - query_id // width
    code = jnp.where((delta_col >= -3) & (delta_col <= 3), delta_row * 8 + delta_col, 1000)

    def mark(index, hit):
        wanted = offset_ref[index, 0] * 8 + offset_ref[index, 1]
        return jnp.where(code == wanted, 0.0, hit)

    bias[...] = lax.fori_loop(
        0, offset_ref.shape[0], mark, jnp.full((tokens, tokens), negative_big, jnp.float32), unroll=True
    )

    def lanes(index):
        return pl.ds(pl.multiple_of(index * HD, HD), HD)

    def scores(role, lag):
        allow = lag_allowed(mask_ref, clip_ref, own, frames, lag)
        shut = jnp.where(allow == 1, 0.0, negative_big).astype(jnp.float32)

        def head(h, _):
            group = h // GROUP
            key = kv[role, :, lanes(group)]
            value = kv[role, :, lanes(HK + group)]
            logit = lax.dot_general(
                key, query_ref[:, lanes(h)], (((1,), (1,)), ((), ())), preferred_element_type=jnp.float32
            )
            dot = lax.dot_general(
                value, cot_ref[:, lanes(h)], (((1,), (1,)), ((), ())), preferred_element_type=jnp.float32
            )
            logit = logit * (SCALE * LOG2E) + (bias[...] + shut)
            top = jnp.max(logit, axis=0, keepdims=True)
            weight = jnp.exp2(logit - top)
            probs[role, h] = weight
            dots[role, h] = dot
            tops[role, h] = top
            sums[role, h] = jnp.sum(weight, axis=0, keepdims=True)
            means[role, h] = jnp.sum(weight * dot, axis=0, keepdims=True)
            return 0

        lax.fori_loop(0, HQ, head, 0, unroll=2)

    lag_second = jnp.where(core == 0, 3, 1)
    lag_relay = jnp.where(core == 0, 1, 3)
    scores(0, jnp.int32(0))
    send_two.wait_recv()
    relay.start()
    scores(2, jnp.int32(2))
    send_one.wait_recv()
    scores(1, lag_second)
    relay.wait_recv()
    scores(3, lag_relay)

    def finish(h, _):
        top = jnp.maximum(jnp.maximum(tops[0, h], tops[1, h]), jnp.maximum(tops[2, h], tops[3, h]))
        factors = [jnp.exp2(tops[role, h] - top) for role in range(4)]
        total = sum(factors[role] * sums[role, h] for role in range(4))
        dot = sum(factors[role] * means[role, h] for role in range(4))
        for role in range(4):
            tops[role, h] = factors[role] / total
        means[0, h] = dot / total
        return 0

    lax.fori_loop(0, HQ, finish, 0)

    def gradients(role, first, store):
        def one_group(group, _):
            key_turned = kv[role, :, lanes(group)].T
            key_sum = None
            value_sum = None
            for a in range(GROUP):
                h = group * GROUP + a
                prob = probs[role, h] * tops[role, h]
                score = (prob * (dots[role, h] - means[0, h])).astype(jnp.bfloat16)
                key_part = jnp.dot(score, query_ref[:, lanes(h)], preferred_element_type=jnp.float32)
                value_part = jnp.dot(
                    prob.astype(jnp.bfloat16), cot_ref[:, lanes(h)], preferred_element_type=jnp.float32
                )
                turned = jnp.dot(key_turned, score, preferred_element_type=jnp.float32)
                key_sum = key_part if a == 0 else key_sum + key_part
                value_sum = value_part if a == 0 else value_sum + value_part
                dq_acc[h] = turned if first else dq_acc[h] + turned
            store(group, key_sum * SCALE, value_sum)
            return 0

        lax.fori_loop(0, HK, one_group, 0)

    def store_out(role):
        def store(group, key_sum, value_sum):
            grads[role, :, lanes(group)] = key_sum.astype(jnp.bfloat16)
            grads[role, :, lanes(HK + group)] = value_sum.astype(jnp.bfloat16)

        return store

    back_relay = remote(3, grads.at[2], arrived.at[2], partner)
    back_two = remote(4, grads.at[1], arrived.at[1], behind)
    back_one = remote(5, grads.at[0], arrived.at[0], second_back)
    gradients(3, True, store_out(2))
    back_relay.start()

    def store_two(group, key_sum, value_sum):
        grads[1, :, lanes(group)] = key_sum.astype(jnp.bfloat16)
        grads[1, :, lanes(HK + group)] = value_sum.astype(jnp.bfloat16)

    gradients(2, False, store_two)
    back_relay.wait_recv()
    grads[1] = (grads[1].astype(jnp.float32) + arrived[2].astype(jnp.float32)).astype(jnp.bfloat16)
    back_two.start()
    gradients(1, False, store_out(0))
    back_one.start()

    def store_own(group, key_sum, value_sum):
        dk_ref[:, lanes(group)] = key_sum
        dv_ref[:, lanes(group)] = value_sum

    gradients(0, False, store_own)

    def query_out(h, _):
        dq_ref[:, lanes(h)] = dq_acc[h].T * SCALE
        return 0

    lax.fori_loop(0, HQ, query_out, 0, unroll=2)
    back_two.wait_recv()
    back_one.wait_recv()
    came = arrived[0].astype(jnp.float32) + arrived[1].astype(jnp.float32)
    dk_ref[...] = dk_ref[...] + came[:, :heads_wide]
    dv_ref[...] = dv_ref[...] + came[:, heads_wide:]
    for copy in (send_two, send_one, relay, back_relay, back_two, back_one):
        copy.wait_send()


def fused_body(queries, keys, values, grad_out, frame_mask, clip_frames, offsets):
    _, rows, width, wide = queries.shape
    tokens = rows * width
    narrow = keys.shape[3]
    frames = lax.axis_size("tm")

    def flat(array):
        return array.reshape(tokens, array.shape[3])

    smem = pl.BlockSpec(memory_space=pltpu.SMEM)
    vmem = pl.BlockSpec(memory_space=pltpu.VMEM)

    def kernel(*refs):
        fused(width, frames, *refs)

    dq, dk, dv = pl.pallas_call(
        kernel,
        out_shape=(
            jax.ShapeDtypeStruct((tokens, wide), jnp.float32),
            jax.ShapeDtypeStruct((tokens, narrow), jnp.float32),
            jax.ShapeDtypeStruct((tokens, narrow), jnp.float32),
        ),
        in_specs=[smem] * 3 + [vmem] * 4,
        out_specs=(vmem, vmem, vmem),
        scratch_shapes=[
            pltpu.VMEM((4, tokens, 2 * narrow), jnp.bfloat16),
            pltpu.VMEM((3, tokens, 2 * narrow), jnp.bfloat16),
            pltpu.VMEM((3, tokens, 2 * narrow), jnp.bfloat16),
            pltpu.VMEM((tokens, tokens), jnp.float32),
            pltpu.VMEM((4, HQ, tokens, tokens), jnp.float32),
            pltpu.VMEM((4, HQ, tokens, tokens), jnp.float32),
            pltpu.VMEM((4, HQ, 1, tokens), jnp.float32),
            pltpu.VMEM((4, HQ, 1, tokens), jnp.float32),
            pltpu.VMEM((4, HQ, 1, tokens), jnp.float32),
            pltpu.VMEM((HQ, HD, tokens), jnp.float32),
            pltpu.SemaphoreType.DMA((6,)),
            pltpu.SemaphoreType.DMA((6,)),
        ],
        compiler_params=pltpu.CompilerParams(
            collective_id=0, has_side_effects=True, vmem_limit_bytes=48 * 1024 * 1024
        ),
    )(frame_mask, clip_frames, offsets, flat(queries), flat(keys), flat(values), flat(grad_out))
    shape = (1, rows, width)
    return dq.reshape(shape + (wide,)), dk.reshape(shape + (narrow,)), dv.reshape(shape + (narrow,))


def solution(mesh):
    whole_rows = mesh.shape["rows"] == 1 and mesh.shape["tm"] % 2 == 0 and mesh.shape["tm"] > 6
    return jax.shard_map(
        fused_body if whole_rows else body,
        mesh=mesh,
        in_specs=(
            P(("groups", "tm"), "rows", None, None),
            P(("groups", "tm"), "rows", None, None),
            P(("groups", "tm"), "rows", None, None),
            P(("groups", "tm"), "rows", None, None),
            P("groups", None),
            P("groups"),
            P(),
        ),
        out_specs=(
            P(("groups", "tm"), "rows", None, None),
            P(("groups", "tm"), "rows", None, None),
            P(("groups", "tm"), "rows", None, None),
        ),
        check_vma=False,
    )
```

profile of v0, /device:TPU:1, one launch (start us, length us, event | category | flops | bytes accessed | tf_op | source)
XLA Modules:
  0.0 40.6 jit_solution(8900219478710121093)
XLA Ops:
  0.6 0.0 copy-start.6
  0.6 0.0 copy-start.4
  0.7 0.7 %copy-done.6 = s32[24,2]{0,1:T(2,128)S(1)} copy-done((s32[24,2]{0,1:T(2,128)S(1)}, s32[24,2]{0,1:T(2,128)}, u32[]{:S(2)}) %copy-start.6) | copy-done | bytes 216
  1.3 0.0 copy-start.5
  1.3 0.1 copy.10.refs_2_
  1.4 0.0 copy-done.4
  1.4 0.6 %copy-done.5 = s32[6]{0:T(128)S(1)} copy-done((s32[6]{0:T(128)S(1)}, s32[6]{0:T(128)}, u32[]{:S(2)}) %copy-start.5) | copy-done | bytes 48
  2.0 0.0 copy-start
  2.0 1.0 %copy-done = bf16[1,4,64,1024]{3,2,1,0:T(8,128)(2,1)S(1)} copy-done((bf16[1,4,64,1024]{3,2,1,0:T(8,128)(2,1)S(1)}, bf16[1,4,64,1024]{3,2,1,0:T(8,128)(2,1)}, u32[]{:S(2)}) %copy-start) | copy-done | bytes 524312
  3.0 0.0 copy-start.1
  3.0 1.0 %copy-done.1 = bf16[1,4,64,1024]{3,2,1,0:T(8,128)(2,1)S(1)} copy-done((bf16[1,4,64,1024]{3,2,1,0:T(8,128)(2,1)S(1)}, bf16[1,4,64,1024]{3,2,1,0:T(8,128)(2,1)}, u32[]{:S(2)}) %copy-start.1) | copy-done | bytes 524312
  4.1 0.0 copy-start.2
  4.1 0.9 %copy-done.2 = bf16[1,4,64,256]{3,2,1,0:T(8,128)(2,1)S(1)} copy-done((bf16[1,4,64,256]{3,2,1,0:T(8,128)(2,1)S(1)}, bf16[1,4,64,256]{3,2,1,0:T(8,128)(2,1)}, u32[]{:S(2)}) %copy-start.2) | copy-done | bytes 131096
  5.0 0.0 copy-start.3
  5.0 0.9 %copy-done.3 = bf16[1,4,64,256]{3,2,1,0:T(8,128)(2,1)S(1)} copy-done((bf16[1,4,64,256]{3,2,1,0:T(8,128)(2,1)S(1)}, bf16[1,4,64,256]{3,2,1,0:T(8,128)(2,1)}, u32[]{:S(2)}) %copy-start.3) | copy-done | bytes 131096
  5.9 32.3 %shard_map.94 = (f32[256,1024]{1,0:T(8,128)S(1)}, f32[256,256]{1,0:T(8,128)S(1)}, f32[256,256]{1,0:T(8,128)S(1)}) custom-call(s32[16,16]{1,0:T(8,128)S(1)} %copy-done.4, s32[6]{0:T(128)S(1)} %copy-done.5, s32[24,2]{1,0:T(8,128)S(1)} %copy.10.refs_2_, bf16[256,1024]{1,0:T(8,128)(2,1)S(1)} %bitcast.8, bf16[256,256]{1,0:T(8,128)(2,1)S(1)} %bitcast.12, ...), custom_call_target="tpu_custom_call" | custom-call | tf_op jit(solution)/shard_map/pallas_call | solution.py:450
  38.2 1.0 %copy.14 = f32[1,4,64,1024]{3,2,1,0:T(8,128)} copy(f32[1,4,64,1024]{3,2,1,0:T(8,128)S(1)} %bitcast.7) | data formatting | bytes 2097152
  39.2 0.7 %copy.15 = f32[1,4,64,256]{3,2,1,0:T(8,128)} copy(f32[1,4,64,256]{3,2,1,0:T(8,128)S(1)} %bitcast.11) | data formatting | bytes 524288
  39.9 0.7 %copy.16 = f32[1,4,64,256]{3,2,1,0:T(8,128)} copy(f32[1,4,64,256]{3,2,1,0:T(8,128)S(1)} %bitcast.10) | data formatting | bytes 524288
Async XLA Ops:
  0.6 0.7 %copy-start.6 = (s32[24,2]{0,1:T(2,128)S(1)}, s32[24,2]{0,1:T(2,128)}, u32[]{:S(2)}) copy-start(s32[24,2]{0,1:T(2,128)} %param.13) | copy-start | bytes 580
  0.6 0.8 %copy-start.4 = (s32[16,16]{1,0:T(8,128)S(1)}, s32[16,16]{1,0:T(8,128)}, u32[]{:S(2)}) copy-start(s32[16,16]{1,0:T(8,128)} %refs_0_.1) | copy-start | bytes 3076
  1.3 0.7 %copy-start.5 = (s32[6]{0:T(128)S(1)}, s32[6]{0:T(128)}, u32[]{:S(2)}) copy-start(s32[6]{0:T(128)} %refs_1_.1) | copy-start | bytes 76
  2.0 1.0 %copy-start = (bf16[1,4,64,1024]{3,2,1,0:T(8,128)(2,1)S(1)}, bf16[1,4,64,1024]{3,2,1,0:T(8,128)(2,1)}, u32[]{:S(2)}) copy-start(bf16[1,4,64,1024]{3,2,1,0:T(8,128)(2,1)} %param.7) | copy-start | bytes 1572868
  3.0 1.0 %copy-start.1 = (bf16[1,4,64,1024]{3,2,1,0:T(8,128)(2,1)S(1)}, bf16[1,4,64,1024]{3,2,1,0:T(8,128)(2,1)}, u32[]{:S(2)}) copy-start(bf16[1,4,64,1024]{3,2,1,0:T(8,128)(2,1)} %param.10) | copy-start | bytes 1572868
  4.1 0.9 %copy-start.2 = (bf16[1,4,64,256]{3,2,1,0:T(8,128)(2,1)S(1)}, bf16[1,4,64,256]{3,2,1,0:T(8,128)(2,1)}, u32[]{:S(2)}) copy-start(bf16[1,4,64,256]{3,2,1,0:T(8,128)(2,1)} %param.8) | copy-start | bytes 393220
  5.0 0.9 %copy-start.3 = (bf16[1,4,64,256]{3,2,1,0:T(8,128)(2,1)S(1)}, bf16[1,4,64,256]{3,2,1,0:T(8,128)(2,1)}, u32[]{:S(2)}) copy-start(bf16[1,4,64,256]{3,2,1,0:T(8,128)(2,1)} %param.9) | copy-start | bytes 393220
where the time goes:
time: 40.9 us; the launch traced here: 40.6 us
  Pallas kernels  32.3 us (79%)
  local copies, waits for them, and re-layouts  7.58 us (19%)
  between operations  0.66 us (2%)
    pallas_call x1, Pallas kernels, fused_body(): pl.pallas_call(kernel, out_shape=(jax.ShapeDtypeStruct((tokens, wide), jn...  32.3 us
    unnamed x18, local copies, waits for them, and re-layouts  7.58 us

commit v1 on v0

--- a/solution.py
+++ b/solution.py
@@ -263,12 +263,24 @@
 
 def fused(
     width, frames,
-    mask_ref, clip_ref, offset_ref, query_ref, key_ref, value_ref, cot_ref,
+    mask_hbm, clip_hbm, offset_hbm, query_hbm, key_hbm, value_hbm, cot_hbm,
     dq_ref, dk_ref, dv_ref,
-    kv, grads, arrived, bias, probs, dots, tops, sums, means, dq_acc, send_sem, recv_sem,
+    mask_ref, clip_ref, offset_ref, query_ref, cot_ref, kv, grads, arrived, bias, probs, dots, tops, sums, means, dq_acc, load_sem, send_sem, recv_sem,
 ):
     tokens = query_ref.shape[0]
     heads_wide = HK * HD
+    pairs = (
+        (key_hbm, kv.at[0, :, pl.ds(0, heads_wide)]),
+        (value_hbm, kv.at[0, :, pl.ds(heads_wide, heads_wide)]),
+        (offset_hbm, offset_ref),
+        (clip_hbm, clip_ref),
+        (mask_hbm, mask_ref),
+        (query_hbm, query_ref),
+        (cot_hbm, cot_ref),
+    )
+    loads = [pltpu.make_async_copy(pair[0], pair[1], load_sem.at[i]) for i, pair in enumerate(pairs)]
+    for load in loads:
+        load.start()
     own = lax.axis_index("tm")
     core = lax.rem(own, 2)
 
@@ -284,8 +296,8 @@
     barrier = pltpu.get_barrier_semaphore()
     for peer in (partner, ahead, behind, far):
         pl.semaphore_signal(barrier, inc=1, device_id=peer, device_id_type=MESH)
-    kv[0, :, :heads_wide] = key_ref[...]
-    kv[0, :, heads_wide:] = value_ref[...]
+    for load in loads[:2]:
+        load.wait()
     pl.semaphore_wait(barrier, 4)
 
     def remote(index, source, target, peer):
@@ -298,7 +310,8 @@
     send_one = remote(1, kv.at[0], kv.at[1], second_to)
     relay = remote(2, kv.at[2], kv.at[3], partner)
     send_two.start()
-    send_one.start()
+    for load in loads[2:]:
+        load.wait()
 
     key_id = lax.broadcasted_iota(jnp.int32, (tokens, tokens), 0)
     query_id = lax.broadcasted_iota(jnp.int32, (tokens, tokens), 1)
@@ -307,11 +320,11 @@
     code = jnp.where((delta_col >= -3) & (delta_col <= 3), delta_row * 8 + delta_col, 1000)
 
     def mark(index, hit):
-        wanted = offset_ref[index, 0] * 8 + offset_ref[index, 1]
+        wanted = offset_ref[0, index] * 8 + offset_ref[1, index]
         return jnp.where(code == wanted, 0.0, hit)
 
     bias[...] = lax.fori_loop(
-        0, offset_ref.shape[0], mark, jnp.full((tokens, tokens), negative_big, jnp.float32), unroll=True
+        0, offset_ref.shape[1], mark, jnp.full((tokens, tokens), negative_big, jnp.float32), unroll=True
     )
 
     def lanes(index):
@@ -341,18 +354,20 @@
             means[role, h] = jnp.sum(weight * dot, axis=0, keepdims=True)
             return 0
 
-        lax.fori_loop(0, HQ, head, 0, unroll=2)
+        lax.fori_loop(0, HQ, head, 0, unroll=4)
 
     lag_second = jnp.where(core == 0, 3, 1)
     lag_relay = jnp.where(core == 0, 1, 3)
     scores(0, jnp.int32(0))
+    send_two.wait_send()
+    send_one.start()
     send_two.wait_recv()
     relay.start()
     scores(2, jnp.int32(2))
+    relay.wait_recv()
+    scores(3, lag_relay)
     send_one.wait_recv()
     scores(1, lag_second)
-    relay.wait_recv()
-    scores(3, lag_relay)
 
     def finish(h, _):
         top = jnp.maximum(jnp.maximum(tops[0, h], tops[1, h]), jnp.maximum(tops[2, h], tops[3, h]))
@@ -400,6 +415,8 @@
     back_one = remote(5, grads.at[0], arrived.at[0], second_back)
     gradients(3, True, store_out(2))
     back_relay.start()
+    gradients(1, False, store_out(0))
+    back_one.start()
 
     def store_two(group, key_sum, value_sum):
         grads[1, :, lanes(group)] = key_sum.astype(jnp.bfloat16)
@@ -409,8 +426,6 @@
     back_relay.wait_recv()
     grads[1] = (grads[1].astype(jnp.float32) + arrived[2].astype(jnp.float32)).astype(jnp.bfloat16)
     back_two.start()
-    gradients(1, False, store_out(0))
-    back_one.start()
 
     def store_own(group, key_sum, value_sum):
         dk_ref[:, lanes(group)] = key_sum
@@ -422,13 +437,13 @@
         dq_ref[:, lanes(h)] = dq_acc[h].T * SCALE
         return 0
 
-    lax.fori_loop(0, HQ, query_out, 0, unroll=2)
+    lax.fori_loop(0, HQ, query_out, 0, unroll=4)
     back_two.wait_recv()
     back_one.wait_recv()
     came = arrived[0].astype(jnp.float32) + arrived[1].astype(jnp.float32)
     dk_ref[...] = dk_ref[...] + came[:, :heads_wide]
     dv_ref[...] = dv_ref[...] + came[:, heads_wide:]
-    for copy in (send_two, send_one, relay, back_relay, back_two, back_one):
+    for copy in (send_one, relay, back_relay, back_two, back_one):
         copy.wait_send()
 
 
@@ -441,7 +456,7 @@
     def flat(array):
         return array.reshape(tokens, array.shape[3])
 
-    smem = pl.BlockSpec(memory_space=pltpu.SMEM)
+    hbm = pl.BlockSpec(memory_space=pltpu.HBM)
     vmem = pl.BlockSpec(memory_space=pltpu.VMEM)
 
     def kernel(*refs):
@@ -454,9 +469,14 @@
             jax.ShapeDtypeStruct((tokens, narrow), jnp.float32),
             jax.ShapeDtypeStruct((tokens, narrow), jnp.float32),
         ),
-        in_specs=[smem] * 3 + [vmem] * 4,
+        in_specs=[hbm] * 7,
         out_specs=(vmem, vmem, vmem),
         scratch_shapes=[
+            pltpu.SMEM(frame_mask.shape, jnp.int32),
+            pltpu.SMEM(clip_frames.shape, jnp.int32),
+            pltpu.SMEM(offsets.shape[::-1], jnp.int32),
+            pltpu.VMEM((tokens, wide), jnp.bfloat16),
+            pltpu.VMEM((tokens, wide), jnp.bfloat16),
             pltpu.VMEM((4, tokens, 2 * narrow), jnp.bfloat16),
             pltpu.VMEM((3, tokens, 2 * narrow), jnp.bfloat16),
             pltpu.VMEM((3, tokens, 2 * narrow), jnp.bfloat16),
@@ -467,13 +487,14 @@
             pltpu.VMEM((4, HQ, 1, tokens), jnp.float32),
             pltpu.VMEM((4, HQ, 1, tokens), jnp.float32),
             pltpu.VMEM((HQ, HD, tokens), jnp.float32),
+            pltpu.SemaphoreType.DMA((7,)),
             pltpu.SemaphoreType.DMA((6,)),
             pltpu.SemaphoreType.DMA((6,)),
         ],
         compiler_params=pltpu.CompilerParams(
             collective_id=0, has_side_effects=True, vmem_limit_bytes=48 * 1024 * 1024
         ),
-    )(frame_mask, clip_frames, offsets, flat(queries), flat(keys), flat(values), flat(grad_out))
+    )(frame_mask, clip_frames, offsets.T, flat(queries), flat(keys), flat(values), flat(grad_out))
     shape = (1, rows, width)
     return dq.reshape(shape + (wide,)), dk.reshape(shape + (narrow,)), dv.reshape(shape + (narrow,))
 

time: 40.9 us -> 37.7 us (0.922)
  the two profiles are of different devices: /device:TPU:1 before, /device:TPU:0 now
where the time goes in v1:
time: 37.7 us; the launch traced here: 37.3 us
  Pallas kernels  29.1 us (77%)
  local copies, waits for them, and re-layouts  7.61 us (20%)
  between operations  0.66 us (2%)
    pallas_call x1, Pallas kernels, fused_body(): pl.pallas_call(kernel, out_shape=(jax.ShapeDtypeStruct((tokens, wide), jn...  29.1 us
    unnamed x17, local copies, waits for them, and re-layouts  7.61 us

profile of v1, /device:TPU:0, one launch (start us, length us, event | category | flops | bytes accessed | tf_op | source)
XLA Modules:
  0.0 37.3 jit_solution(14692920755375591645)
XLA Ops:
  0.6 0.0 copy-start.4
  0.6 0.0 copy-start.5
  0.7 0.7 %copy-done.4 = s32[16,16]{1,0:T(8,128)S(1)} copy-done((s32[16,16]{1,0:T(8,128)S(1)}, s32[16,16]{1,0:T(8,128)}, u32[]{:S(2)}) %copy-start.4) | copy-done | bytes 1048
  1.3 0.0 copy-done.5
  1.3 0.0 copy-start
  1.3 1.0 %copy-done = bf16[1,4,64,1024]{3,2,1,0:T(8,128)(2,1)S(1)} copy-done((bf16[1,4,64,1024]{3,2,1,0:T(8,128)(2,1)S(1)}, bf16[1,4,64,1024]{3,2,1,0:T(8,128)(2,1)}, u32[]{:S(2)}) %copy-start) | copy-done | bytes 524312
  2.4 0.0 copy-start.1
  2.4 1.0 %copy-done.1 = bf16[1,4,64,1024]{3,2,1,0:T(8,128)(2,1)S(1)} copy-done((bf16[1,4,64,1024]{3,2,1,0:T(8,128)(2,1)S(1)}, bf16[1,4,64,1024]{3,2,1,0:T(8,128)(2,1)}, u32[]{:S(2)}) %copy-start.1) | copy-done | bytes 524312
  3.4 0.0 copy-start.2
  3.4 0.9 %copy-done.2 = bf16[1,4,64,256]{3,2,1,0:T(8,128)(2,1)S(1)} copy-done((bf16[1,4,64,256]{3,2,1,0:T(8,128)(2,1)S(1)}, bf16[1,4,64,256]{3,2,1,0:T(8,128)(2,1)}, u32[]{:S(2)}) %copy-start.2) | copy-done | bytes 131096
  4.3 0.0 copy-start.3
  4.3 0.9 %copy-done.3 = bf16[1,4,64,256]{3,2,1,0:T(8,128)(2,1)S(1)} copy-done((bf16[1,4,64,256]{3,2,1,0:T(8,128)(2,1)S(1)}, bf16[1,4,64,256]{3,2,1,0:T(8,128)(2,1)}, u32[]{:S(2)}) %copy-start.3) | copy-done | bytes 131096
  5.2 0.0 copy-start.6
  5.2 0.7 %copy-done.6 = s32[6]{0:T(128)S(1)} copy-done((s32[6]{0:T(128)S(1)}, s32[6]{0:T(128)}, u32[]{:S(2)}) %copy-start.6) | copy-done | bytes 48
  5.9 29.1 %shard_map.94 = (f32[256,1024]{1,0:T(8,128)S(1)}, f32[256,256]{1,0:T(8,128)S(1)}, f32[256,256]{1,0:T(8,128)S(1)}) custom-call(s32[16,16]{1,0:T(8,128)S(1)} %copy-done.4, s32[6]{0:T(128)S(1)} %copy-done.6, s32[2,24]{1,0:T(2,128)S(1)} %bitcast.15, bf16[256,1024]{1,0:T(8,128)(2,1)S(1)} %bitcast.9, bf16[256,256]{1,0:T(8,128)(2,1)S(1)} %bitcast.13, ...), custom_call_target="tpu_custom_call" | custom-call | tf_op jit(solution)/shard_map/pallas_call | solution.py:465
  35.0 1.0 %copy.13 = f32[1,4,64,1024]{3,2,1,0:T(8,128)} copy(f32[1,4,64,1024]{3,2,1,0:T(8,128)S(1)} %bitcast.8) | data formatting | bytes 2097152
  35.9 0.7 %copy.14 = f32[1,4,64,256]{3,2,1,0:T(8,128)} copy(f32[1,4,64,256]{3,2,1,0:T(8,128)S(1)} %bitcast.12) | data formatting | bytes 524288
  36.6 0.7 %copy.15 = f32[1,4,64,256]{3,2,1,0:T(8,128)} copy(f32[1,4,64,256]{3,2,1,0:T(8,128)S(1)} %bitcast.11) | data formatting | bytes 524288
Async XLA Ops:
  0.6 0.7 %copy-start.4 = (s32[16,16]{1,0:T(8,128)S(1)}, s32[16,16]{1,0:T(8,128)}, u32[]{:S(2)}) copy-start(s32[16,16]{1,0:T(8,128)} %refs_0_.1) | copy-start | bytes 3076
  0.6 0.7 %copy-start.5 = (s32[24,2]{0,1:T(2,128)S(1)}, s32[24,2]{0,1:T(2,128)}, u32[]{:S(2)}) copy-start(s32[24,2]{0,1:T(2,128)} %param.13) | copy-start | bytes 580
  1.3 1.0 %copy-start = (bf16[1,4,64,1024]{3,2,1,0:T(8,128)(2,1)S(1)}, bf16[1,4,64,1024]{3,2,1,0:T(8,128)(2,1)}, u32[]{:S(2)}) copy-start(bf16[1,4,64,1024]{3,2,1,0:T(8,128)(2,1)} %param.7) | copy-start | bytes 1572868
  2.4 1.0 %copy-start.1 = (bf16[1,4,64,1024]{3,2,1,0:T(8,128)(2,1)S(1)}, bf16[1,4,64,1024]{3,2,1,0:T(8,128)(2,1)}, u32[]{:S(2)}) copy-start(bf16[1,4,64,1024]{3,2,1,0:T(8,128)(2,1)} %param.10) | copy-start | bytes 1572868
  3.4 0.9 %copy-start.2 = (bf16[1,4,64,256]{3,2,1,0:T(8,128)(2,1)S(1)}, bf16[1,4,64,256]{3,2,1,0:T(8,128)(2,1)}, u32[]{:S(2)}) copy-start(bf16[1,4,64,256]{3,2,1,0:T(8,128)(2,1)} %param.8) | copy-start | bytes 393220
  4.3 0.9 %copy-start.3 = (bf16[1,4,64,256]{3,2,1,0:T(8,128)(2,1)S(1)}, bf16[1,4,64,256]{3,2,1,0:T(8,128)(2,1)}, u32[]{:S(2)}) copy-start(bf16[1,4,64,256]{3,2,1,0:T(8,128)(2,1)} %param.9) | copy-start | bytes 393220
  5.2 0.7 %copy-start.6 = (s32[6]{0:T(128)S(1)}, s32[6]{0:T(128)}, u32[]{:S(2)}) copy-start(s32[6]{0:T(128)} %refs_1_.1) | copy-start | bytes 76

commit v2 on v1

--- a/solution.py
+++ b/solution.py
@@ -264,8 +264,8 @@
 def fused(
     width, frames,
     mask_hbm, clip_hbm, offset_hbm, query_hbm, key_hbm, value_hbm, cot_hbm,
-    dq_ref, dk_ref, dv_ref,
-    mask_ref, clip_ref, offset_ref, query_ref, cot_ref, kv, grads, arrived, bias, probs, dots, tops, sums, means, dq_acc, load_sem, send_sem, recv_sem,
+    dq_hbm, dk_ref, dv_ref,
+    dq_ref, mask_ref, clip_ref, offset_ref, query_ref, cot_ref, kv, grads, arrived, bias, probs, dots, tops, sums, means, dq_acc, load_sem, send_sem, recv_sem,
 ):
     tokens = query_ref.shape[0]
     heads_wide = HK * HD
@@ -438,6 +438,8 @@
         return 0
 
     lax.fori_loop(0, HQ, query_out, 0, unroll=4)
+    store_queries = pltpu.make_async_copy(dq_ref, dq_hbm, load_sem.at[7])
+    store_queries.start()
     back_two.wait_recv()
     back_one.wait_recv()
     came = arrived[0].astype(jnp.float32) + arrived[1].astype(jnp.float32)
@@ -445,6 +447,7 @@
     dv_ref[...] = dv_ref[...] + came[:, heads_wide:]
     for copy in (send_one, relay, back_relay, back_two, back_one):
         copy.wait_send()
+    store_queries.wait()
 
 
 def fused_body(queries, keys, values, grad_out, frame_mask, clip_frames, offsets):
@@ -470,8 +473,9 @@
             jax.ShapeDtypeStruct((tokens, narrow), jnp.float32),
         ),
         in_specs=[hbm] * 7,
-        out_specs=(vmem, vmem, vmem),
+        out_specs=(hbm, vmem, vmem),
         scratch_shapes=[
+            pltpu.VMEM((tokens, wide), jnp.float32),
             pltpu.SMEM(frame_mask.shape, jnp.int32),
             pltpu.SMEM(clip_frames.shape, jnp.int32),
             pltpu.SMEM(offsets.shape[::-1], jnp.int32),
@@ -487,12 +491,12 @@
             pltpu.VMEM((4, HQ, 1, tokens), jnp.float32),
             pltpu.VMEM((4, HQ, 1, tokens), jnp.float32),
             pltpu.VMEM((HQ, HD, tokens), jnp.float32),
-            pltpu.SemaphoreType.DMA((7,)),
+            pltpu.SemaphoreType.DMA((8,)),
             pltpu.SemaphoreType.DMA((6,)),
             pltpu.SemaphoreType.DMA((6,)),
         ],
         compiler_params=pltpu.CompilerParams(
-            collective_id=0, has_side_effects=True, vmem_limit_bytes=48 * 1024 * 1024
+            collective_id=0, has_side_effects=True, vmem_limit_bytes=63 * 1024 * 1024 - 65536
         ),
     )(frame_mask, clip_frames, offsets.T, flat(queries), flat(keys), flat(values), flat(grad_out))
     shape = (1, rows, width)

time: 37.7 us -> 35.2 us (0.934)
  local copies, waits for them, and re-layouts: 7.61 us -> 4.1 us
  Pallas kernels: 29.1 us -> 30.2 us
    unnamed x17 -> x7, local copies, waits for them, and re-layouts: 7.61 us -> 4.1 us
    pallas_call x1, Pallas kernels: 29.1 us -> 30.2 us  [fused_body(): pl.pallas_call(kernel, out_shape=(jax.ShapeDtypeStruct((tokens, wide), jn...]
where the time goes in v2:
time: 35.2 us; the launch traced here: 35 us
  Pallas kernels  30.2 us (86%)
  local copies, waits for them, and re-layouts  4.1 us (12%)
  between operations  0.65 us (2%)
    pallas_call x1, Pallas kernels, fused_body(): pl.pallas_call(kernel, out_shape=(jax.ShapeDtypeStruct((tokens, wide), jn...  30.2 us
    unnamed x7, local copies, waits for them, and re-layouts  4.1 us

profile of v2, /device:TPU:0, one launch (start us, length us, event | category | flops | bytes accessed | tf_op | source)
XLA Modules:
  0.0 35.0 jit_solution(2359133630241673210)
XLA Ops:
  0.6 30.2 %shard_map.94 = (f32[256,1024]{1,0:T(8,128)}, f32[256,256]{1,0:T(8,128)}, f32[256,256]{1,0:T(8,128)}) custom-call(s32[16,16]{1,0:T(8,128)} %refs_0_.1, s32[6]{0:T(128)} %refs_1_.1, s32[2,24]{1,0:T(2,128)} %bitcast.15, bf16[256,1024]{1,0:T(8,128)(2,1)} %bitcast.9, bf16[256,256]{1,0:T(8,128)(2,1)} %bitcast.13, bf16[256,256]{1,0:T(8,128)(2,1)} %bitcast.14, ...), custom_call_target="tpu_custom_call" | custom-call | tf_op jit(solution)/shard_map/pallas_call | solution.py:468
  30.9 0.0 copy-start.1
  30.9 2.3 %copy.13 = f32[1,4,64,1024]{3,2,1,0:T(8,128)} copy(f32[1,4,64,1024]{3,2,1,0:T(8,128)} %bitcast.8) | data formatting | bytes 2097152
  33.2 0.0 copy-done.1
  33.2 0.0 copy-start
  33.2 0.7 %copy.14 = f32[1,4,64,256]{3,2,1,0:T(8,128)} copy(f32[1,4,64,256]{3,2,1,0:T(8,128)S(1)} %bitcast.12) | data formatting | bytes 524288
  33.9 0.3 copy-done
  34.3 0.7 %copy.15 = f32[1,4,64,256]{3,2,1,0:T(8,128)} copy(f32[1,4,64,256]{3,2,1,0:T(8,128)S(1)} %bitcast.11) | data formatting | bytes 524288
Async XLA Ops:
  30.9 2.4 %copy-start.1 = (f32[256,256]{1,0:T(8,128)S(1)}, f32[256,256]{1,0:T(8,128)}, u32[]{:S(2)}) copy-start(f32[256,256]{1,0:T(8,128)} %get-tuple-element.7) | copy-start | bytes 786436
  33.2 1.0 %copy-start = (f32[256,256]{1,0:T(8,128)S(1)}, f32[256,256]{1,0:T(8,128)}, u32[]{:S(2)}) copy-start(f32[256,256]{1,0:T(8,128)} %get-tuple-element.8) | copy-start | bytes 786436

commit v3 on v2

--- a/solution.py
+++ b/solution.py
@@ -264,7 +264,7 @@
 def fused(
     width, frames,
     mask_hbm, clip_hbm, offset_hbm, query_hbm, key_hbm, value_hbm, cot_hbm,
-    dq_hbm, dk_ref, dv_ref,
+    dq_hbm, kv_grads_ref,
     dq_ref, mask_ref, clip_ref, offset_ref, query_ref, cot_ref, kv, grads, arrived, bias, probs, dots, tops, sums, means, dq_acc, load_sem, send_sem, recv_sem,
 ):
     tokens = query_ref.shape[0]
@@ -428,8 +428,8 @@
     back_two.start()
 
     def store_own(group, key_sum, value_sum):
-        dk_ref[:, lanes(group)] = key_sum
-        dv_ref[:, lanes(group)] = value_sum
+        kv_grads_ref[0, :, lanes(group)] = key_sum
+        kv_grads_ref[1, :, lanes(group)] = value_sum
 
     gradients(0, False, store_own)
 
@@ -443,8 +443,8 @@
     back_two.wait_recv()
     back_one.wait_recv()
     came = arrived[0].astype(jnp.float32) + arrived[1].astype(jnp.float32)
-    dk_ref[...] = dk_ref[...] + came[:, :heads_wide]
-    dv_ref[...] = dv_ref[...] + came[:, heads_wide:]
+    kv_grads_ref[0] = kv_grads_ref[0] + came[:, :heads_wide]
+    kv_grads_ref[1] = kv_grads_ref[1] + came[:, heads_wide:]
     for copy in (send_one, relay, back_relay, back_two, back_one):
         copy.wait_send()
     store_queries.wait()
@@ -465,15 +465,14 @@
     def kernel(*refs):
         fused(width, frames, *refs)
 
-    dq, dk, dv = pl.pallas_call(
+    dq, kv_grads = pl.pallas_call(
         kernel,
         out_shape=(
             jax.ShapeDtypeStruct((tokens, wide), jnp.float32),
-            jax.ShapeDtypeStruct((tokens, narrow), jnp.float32),
-            jax.ShapeDtypeStruct((tokens, narrow), jnp.float32),
+            jax.ShapeDtypeStruct((2, tokens, narrow), jnp.float32),
         ),
         in_specs=[hbm] * 7,
-        out_specs=(hbm, vmem, vmem),
+        out_specs=(hbm, vmem),
         scratch_shapes=[
             pltpu.VMEM((tokens, wide), jnp.float32),
             pltpu.SMEM(frame_mask.shape, jnp.int32),
@@ -500,7 +499,7 @@
         ),
     )(frame_mask, clip_frames, offsets.T, flat(queries), flat(keys), flat(values), flat(grad_out))
     shape = (1, rows, width)
-    return dq.reshape(shape + (wide,)), dk.reshape(shape + (narrow,)), dv.reshape(shape + (narrow,))
+    return dq.reshape(shape + (wide,)), kv_grads[0].reshape(shape + (narrow,)), kv_grads[1].reshape(shape + (narrow,))
 
 
 def solution(mesh):

time: 35.2 us -> 33.9 us (0.963)
  local copies, waits for them, and re-layouts: 4.1 us -> 2.91 us
    unnamed x7 -> x3, local copies, waits for them, and re-layouts: 4.1 us -> 0.97 us
    slice x0 -> x1, local copies, waits for them, and re-layouts: none -> 1.94 us  [fused_body(): kv_grads[1].reshape(shape + (narrow,))]
where the time goes in v3:
time: 33.9 us; the launch traced here: 33.8 us
  Pallas kernels  30.2 us (89%)
  local copies, waits for them, and re-layouts  2.91 us (9%)
  between operations  0.65 us (2%)
    pallas_call x1, Pallas kernels, fused_body(): pl.pallas_call(kernel, out_shape=(jax.ShapeDtypeStruct((tokens, wide), jn...  30.2 us
    slice x1, local copies, waits for them, and re-layouts, fused_body(): kv_grads[1].reshape(shape + (narrow,))  1.94 us
    unnamed x3, local copies, waits for them, and re-layouts  0.97 us

profile of v3, /device:TPU:0, one launch (start us, length us, event | category | flops | bytes accessed | tf_op | source)
XLA Modules:
  0.0 33.8 jit_solution(7661722882343705082)
XLA Ops:
  0.6 30.2 %shard_map.94 = (f32[256,1024]{1,0:T(8,128)}, f32[2,256,256]{2,1,0:T(8,128)}) custom-call(s32[16,16]{1,0:T(8,128)} %refs_0_.1, s32[6]{0:T(128)} %refs_1_.1, s32[2,24]{1,0:T(2,128)} %bitcast.15, bf16[256,1024]{1,0:T(8,128)(2,1)} %bitcast.9, bf16[256,256]{1,0:T(8,128)(2,1)} %bitcast.13, bf16[256,256]{1,0:T(8,128)(2,1)} %bitcast.14, bf16[256,1024]{1,0:T(8,128)(2,1)} %bitcast.10), custom_call_target="tpu_custom_call" | custom-call | tf_op jit(solution)/shard_map/pallas_call | solution.py:468
  30.9 0.0 copy-start
  30.9 1.9 %fusion = (f32[1,256,256]{2,1,0:T(8,128)}, f32[1,256,256]{2,1,0:T(8,128)}) fusion(f32[2,256,256]{2,1,0:T(8,128)} %get-tuple-element.6), kind=kLoop, calls=%fused_computation | loop fusion | bytes 1048576 | tf_op jit(solution)/shard_map/slice | solution.py:502
  32.8 0.0 copy-done
  32.8 1.0 %copy.11 = f32[1,4,64,1024]{3,2,1,0:T(8,128)} copy(f32[1,4,64,1024]{3,2,1,0:T(8,128)S(1)} %bitcast.8) | data formatting | bytes 2097152
Async XLA Ops:
  30.9 2.0 %copy-start = (f32[256,1024]{1,0:T(8,128)S(1)}, f32[256,1024]{1,0:T(8,128)}, u32[]{:S(2)}) copy-start(f32[256,1024]{1,0:T(8,128)} %get-tuple-element.5) | copy-start | bytes 3145732

commit v4 on v3

--- a/solution.py
+++ b/solution.py
@@ -279,7 +279,7 @@
         (cot_hbm, cot_ref),
     )
     loads = [pltpu.make_async_copy(pair[0], pair[1], load_sem.at[i]) for i, pair in enumerate(pairs)]
-    for load in loads:
+    for load in loads[:2]:
         load.start()
     own = lax.axis_index("tm")
     core = lax.rem(own, 2)
@@ -310,6 +310,8 @@
     send_one = remote(1, kv.at[0], kv.at[1], second_to)
     relay = remote(2, kv.at[2], kv.at[3], partner)
     send_two.start()
+    for load in loads[2:]:
+        load.start()
     for load in loads[2:]:
         load.wait()
 

time: 33.9 us -> 34 us (level)
  no operation moved by 1% of the time
where the time goes in v4:
time: 34 us; the launch traced here: 33.8 us
  Pallas kernels  30.2 us (89%)
  local copies, waits for them, and re-layouts  2.91 us (9%)
  between operations  0.65 us (2%)
    pallas_call x1, Pallas kernels, fused_body(): pl.pallas_call(kernel, out_shape=(jax.ShapeDtypeStruct((tokens, wide), jn...  30.2 us
    slice x1, local copies, waits for them, and re-layouts, fused_body(): kv_grads[1].reshape(shape + (narrow,))  1.94 us
    unnamed x3, local copies, waits for them, and re-layouts  0.97 us

profile of v4, /device:TPU:0, one launch (start us, length us, event | category | flops | bytes accessed | tf_op | source)
XLA Modules:
  0.0 33.8 jit_solution(14766794723499574930)
XLA Ops:
  0.6 30.2 %shard_map.94 = (f32[256,1024]{1,0:T(8,128)}, f32[2,256,256]{2,1,0:T(8,128)}) custom-call(s32[16,16]{1,0:T(8,128)} %refs_0_.1, s32[6]{0:T(128)} %refs_1_.1, s32[2,24]{1,0:T(2,128)} %bitcast.15, bf16[256,1024]{1,0:T(8,128)(2,1)} %bitcast.9, bf16[256,256]{1,0:T(8,128)(2,1)} %bitcast.13, bf16[256,256]{1,0:T(8,128)(2,1)} %bitcast.14, bf16[256,1024]{1,0:T(8,128)(2,1)} %bitcast.10), custom_call_target="tpu_custom_call" | custom-call | tf_op jit(solution)/shard_map/pallas_call | solution.py:470
  30.9 0.0 copy-start
  30.9 1.9 %fusion = (f32[1,256,256]{2,1,0:T(8,128)}, f32[1,256,256]{2,1,0:T(8,128)}) fusion(f32[2,256,256]{2,1,0:T(8,128)} %get-tuple-element.6), kind=kLoop, calls=%fused_computation | loop fusion | bytes 1048576 | tf_op jit(solution)/shard_map/slice | solution.py:504
  32.8 0.0 copy-done
  32.8 1.0 %copy.11 = f32[1,4,64,1024]{3,2,1,0:T(8,128)} copy(f32[1,4,64,1024]{3,2,1,0:T(8,128)S(1)} %bitcast.8) | data formatting | bytes 2097152
Async XLA Ops:
  30.9 2.0 %copy-start = (f32[256,1024]{1,0:T(8,128)S(1)}, f32[256,1024]{1,0:T(8,128)}, u32[]{:S(2)}) copy-start(f32[256,1024]{1,0:T(8,128)} %get-tuple-element.5) | copy-start | bytes 3145732
